TPU v7x, 512 devices: a whole 4x4x16 slice. The times are simulated.
512 devices in a mesh: node: 32 (over y, z_lo), local: 16 (over x, z_hi, core).
Axes of the slice: x: 4, y: 4, z: 16 (z_hi: 2, z_lo: 8; z = z_hi * 8 + z_lo), core: 2. Of those that a mesh axis runs over, the one named last changes fastest.
Arguments:
- tokens: bfloat16 [65536, 4096], P(('node', 'local')), may hold values from -24 to 24
- key_codes: bfloat16 [4096, 512], P('local'), may hold values from -0.09375 to 0.09375
- key_exponents: int32 [4096, 2], P('local'), may hold values from -1 to 1
- key_cotangent: bfloat16 [65536, 512], P(('node', 'local')), may hold values from -6 to 6
Outputs:
- keys: bfloat16 [65536, 512], P(('node', 'local'))
- input_grad: bfloat16 [65536, 4096], P(('node', 'local'))
- weight_grad: float32 [4096, 512], P(('node', 'local'))
Inputs may be any that keep to these rules, and one draw needn't show every extreme that they name: key_exponents gives the power of two that scales each block of 256 columns of a row of key_codes.
All inputs are finite; a program needn't handle non-finite values.
Results may differ from a plain program's by a relative error of at most 0.015.
Values may be sent and summed in bfloat16 or wider, within the bound.
No kernel may reach another device: no remote copies, remote signals or barrier semaphores. Data moves between devices by JAX's collectives and lax.ppermute only.
A program may use at most 128 MiB of HBM per device.

v0:
```python
import math
import jax
import jax.numpy as jnp
from jax import lax
from jax.sharding import PartitionSpec as P

KVH = 4
HEAD = 128
QBLOCK = 256
SEQ = 8192
THETA = 500000.0


def in_blocks(value, dim, size):
    before, after = (value.shape[:dim], value.shape[dim + 1 :])
    return jnp.moveaxis(value.reshape(*before, size, -1, *after), dim, 0)


def joined_along(blocks, dim):
    blocks = jnp.moveaxis(blocks, 0, dim)
    lengths = blocks.shape
    return blocks.reshape(*lengths[:dim], lengths[dim] * lengths[dim + 1], *lengths[dim + 2 :])


def joined_exchange(value, axis, axes, splits, concats):
    sizes = [lax.axis_size(a) for a in axes]
    blocks = in_blocks(value, splits[0], sizes[0])
    blocks = jnp.moveaxis(in_blocks(blocks, splits[1] + 1, sizes[1]), 0, 1)
    inside = blocks.shape[2:]
    blocks = blocks.reshape(-1, *inside)
    blocks = lax.all_to_all(blocks, axis, split_axis=0, concat_axis=0, tiled=True)
    blocks = joined_along(blocks.reshape(*sizes, *inside), concats[0] + 1)
    return joined_along(blocks, concats[1])


def tables(positions):
    inverse = THETA ** (-(jnp.arange(HEAD // 2, dtype=jnp.float32) * 2.0 / HEAD))
    angles = positions.astype(jnp.float32)[:, None] * inverse[None, :]
    return (jnp.cos(angles), jnp.sin(angles))


def rotate(values, cosine, sine_part):
    count = values.shape[0]
    heads = values.reshape(count, KVH, HEAD)
    first_half = heads[:, :, : HEAD // 2]
    second_half = heads[:, :, HEAD // 2 :]
    cos_rows = cosine[:, None, :]
    sin_rows = sine_part[:, None, :]
    joined = jnp.concatenate(
        [
            first_half * cos_rows - second_half * sin_rows,
            second_half * cos_rows + first_half * sin_rows,
        ],
        axis=2,
    )
    return joined.reshape(count, KVH * HEAD)


def unrotate(values, cosine, sine_part):
    count = values.shape[0]
    heads = values.reshape(count, KVH, HEAD)
    first_half = heads[:, :, : HEAD // 2]
    second_half = heads[:, :, HEAD // 2 :]
    cos_rows = cosine[:, None, :]
    sin_rows = sine_part[:, None, :]
    joined = jnp.concatenate(
        [
            first_half * cos_rows + second_half * sin_rows,
            second_half * cos_rows - first_half * sin_rows,
        ],
        axis=2,
    )
    return joined.reshape(count, KVH * HEAD)


def quantize(partial_value):
    blocks = partial_value.reshape(partial_value.shape[0], partial_value.shape[1] // QBLOCK, QBLOCK)
    largest = jnp.max(jnp.abs(blocks), axis=2)
    block_scale = jnp.exp2(jnp.ceil(jnp.log2(largest + 1e-06)))
    code_values = (blocks / block_scale[:, :, None]).astype(jnp.bfloat16)
    return (code_values, block_scale.astype(jnp.bfloat16))


def expand_codes(code_values, block_scale):
    lead = code_values.shape[:-1]
    blocks = code_values.reshape(lead + (block_scale.shape[-1], QBLOCK))
    values = blocks.astype(jnp.float32) * block_scale.astype(jnp.float32)[..., None]
    return values.reshape(lead + (code_values.shape[-1],))


def on_device(tokens, key_codes, key_exponents, key_cotangent):
    node_count = lax.axis_size("node")
    local_count = lax.axis_size("local")
    tok_count = tokens.shape[0]
    width = tokens.shape[1]
    feature_count = key_codes.shape[1]
    expanded = jnp.repeat(jnp.exp2(key_exponents.astype(jnp.float32)), QBLOCK, axis=1)
    shard_weights = (key_codes.astype(jnp.float32) * expanded).astype(jnp.bfloat16)
    weights = lax.all_gather(shard_weights, "local", axis=0, tiled=True)
    device_index = lax.axis_index("node") * local_count + lax.axis_index("local")
    positions = (device_index * tok_count + jnp.arange(tok_count, dtype=jnp.int32)) % SEQ
    cosine, sine_part = tables(positions)
    pre_grad = unrotate(key_cotangent.astype(jnp.float32), cosine, sine_part).astype(jnp.bfloat16)
    partial_value = lax.dot_general(
        tokens, pre_grad, (((0,), (0,)), ((), ())), preferred_element_type=jnp.float32
    )
    code_values, block_scale = quantize(partial_value)
    row_count = width // (node_count * local_count)
    block_count = feature_count // QBLOCK
    code_grid = code_values.reshape(node_count, local_count, row_count, feature_count)
    scale_grid = block_scale.reshape(node_count, local_count, row_count, block_count)
    projected = jnp.dot(tokens, weights, preferred_element_type=jnp.float32)
    keys = rotate(projected, cosine, sine_part).astype(jnp.bfloat16)
    input_grad = lax.dot_general(
        pre_grad, weights, (((1,), (1,)), ((), ())), preferred_element_type=jnp.float32
    ).astype(jnp.bfloat16)
    got_codes, got_scales = (
        joined_exchange(code_grid, ("local", "node"), ("local", "node"), (1, 0), (1, 0)),
        joined_exchange(scale_grid, ("local", "node"), ("local", "node"), (1, 0), (1, 0)),
    )
    summed = jnp.sum(expand_codes(got_codes, got_scales), axis=(0, 1))
    total_tokens = tok_count * node_count * local_count
    weight_grad = summed * (1.0 / math.sqrt(total_tokens))
    return (keys, input_grad, weight_grad)


def solution(mesh):
    return jax.shard_map(
        on_device,
        mesh=mesh,
        in_specs=(
            P(("node", "local"), None),
            P("local", None),
            P("local", None),
            P(("node", "local"), None),
        ),
        out_specs=(
            P(("node", "local"), None),
            P(("node", "local"), None),
            P(("node", "local"), None),
        ),
        check_vma=False,
    )
```

profile of v0, /device:TPU:1, one launch (start us, length us, event | category | flops | bytes accessed | tf_op | source)
XLA Modules:
  0.0 424.3 jit_solution(15492790936828746594)
XLA Ops:
  7.2 0.0 copy-start
  7.2 0.0 all-gather.2.cloned.1.call-start
  7.2 0.8 multiply_exponential_fusion.1
  8.0 0.1 copy.20
  8.1 0.3 broadcast_in_dim.2
  8.5 1.7 multiply_convert_fusion
  10.3 0.0 all-gather.2.cloned.1.call-update
  10.3 1.0 copy.32
  11.3 0.2 multiply_cosine_fusion
  11.5 125.4 %all-gather.2.cloned.1.call-done = bf16[4096,512]{1,0:T(8,128)(2,1)} async-done(((bf16[256,512]{1,0:T(8,128)(2,1)}), bf16[4096,512]{1,0:T(8,128)(2,1)}) %all-gather.2.cloned.1.call-update) | async-done | bytes 4194320 | tf_op jit(solution)/shard_map/all_gather | solution.py:99
  136.9 0.0 copy-done
  136.9 3.5 fusion.6
  140.4 0.1 add_convert_fusion
  140.5 4.5 %bitcast_reduce_fusion = (f32[4096,2]{0,1:T(2,128)S(1)}, f32[4096,512]{0,1:T(8,128)}) fusion(bf16[128,512]{0,1:T(8,128)(2,1)S(1)} %bitcast.48, bf16[128,4096]{1,0:T(8,128)(2,1)S(1)} %copy-done), kind=kOutput, calls=%fused_computation.3 | convolution fusion | flops 541057024 | bytes 9601024 | tf_op jit(solution)/shard_map/dot_general | solution.py:104
  145.0 0.1 fusion.5
  145.1 0.6 copy.25
  145.7 6.0 %div.25 = f32[4096,2,256]{2,1,0:T(2,128)} broadcast(f32[4096,2]{1,0:T(8,128)S(1)} %copy.25), dimensions={0,1} | broadcast | bytes 8421376 | tf_op jit(solution)/shard_map/div | solution.py:80
  151.7 11.5 %div.26 = f32[32,16,1,8,512]{4,3,1,0,2:T(8,128)} reshape(f32[4096,2,256]{2,1,0:T(2,128)} %div.25) | data formatting | bytes 16777216 | tf_op jit(solution)/shard_map/div | solution.py:80
  163.2 9.0 %copy.24 = f32[4096,512]{1,0:T(8,128)} copy(f32[4096,512]{0,1:T(8,128)} %get-tuple-element.14) | data formatting | bytes 16777216 | tf_op jit(solution)/shard_map/dot_general | solution.py:104
  172.2 0.3 reshape.192
  172.5 1.0 copy.31
  173.5 11.5 %all-to-all-start.1 = ((bf16[512,1,1,8,2]{3,4,2,1,0:T(2,128)(2,1)}), bf16[512,1,1,8,2]{3,4,2,1,0:T(2,128)(2,1)S(1)}, u32[]{:S(2)}, u32[]{:S(2)}) async-start(bf16[512,1,1,8,2]{3,4,2,1,0:T(2,128)(2,1)} %bitcast.14), calls=%async_computation.1 | async-start | bytes 524288 | tf_op jit(solution)/shard_map/all_to_all | solution.py:31
  185.0 7.6 %fusion.2 = bf16[16,32,1,8,512]{4,3,0,1,2:T(8,128)(2,1)S(1)} fusion(f32[32,16,1,8,512]{4,3,1,0,2:T(8,128)} %bitcast.43, f32[32,16,1,8,512]{4,3,1,0,2:T(8,128)} %div.26), kind=kLoop, calls=%fused_computation.7 | loop fusion | flops 4194304 | bytes 20971520 | tf_op jit(solution)/shard_map/transpose | solution.py:16
  192.6 2.4 copy.26
  195.0 14.9 %all-to-all-done.1 = bf16[512,1,1,8,2]{3,4,2,1,0:T(2,128)(2,1)S(1)} async-done(((bf16[512,1,1,8,2]{3,4,2,1,0:T(2,128)(2,1)}), bf16[512,1,1,8,2]{3,4,2,1,0:T(2,128)(2,1)S(1)}, u32[]{:S(2)}, u32[]{:S(2)}) %all-to-all-start.1) | async-done | bytes 16416 | tf_op jit(solution)/shard_map/all_to_all | solution.py:31
  210.0 11.3 %all-to-all-start = ((bf16[512,1,1,8,512]{4,3,2,1,0:T(8,128)(2,1)}), bf16[512,1,1,8,512]{4,3,2,1,0:T(8,128)(2,1)}, u32[]{:S(2)}, u32[]{:S(2)}) async-start(bf16[512,1,1,8,512]{4,3,2,1,0:T(8,128)(2,1)} %bitcast.45), calls=%async_computation | async-start | bytes 8388608 | tf_op jit(solution)/shard_map/all_to_all | solution.py:31
  221.3 0.8 copy.30
  222.1 4.7 %convolution_convert_fusion = bf16[128,4096]{1,0:T(8,128)(2,1)} fusion(bf16[128,512]{0,1:T(8,128)(2,1)S(1)} %bitcast.49, bf16[4096,512]{1,0:T(8,128)(2,1)} %all-gather.2.cloned.1.call-done), kind=kOutput, calls=%fused_computation.6 | convolution fusion | flops 537395200 | bytes 5373952 | tf_op jit(solution)/shard_map/dot_general | solution.py:114
  226.7 0.2 convert_bitcast_fusion.1
  226.9 185.2 %all-to-all-done = bf16[512,1,1,8,512]{4,3,2,1,0:T(8,128)(2,1)} async-done(((bf16[512,1,1,8,512]{4,3,2,1,0:T(8,128)(2,1)}), bf16[512,1,1,8,512]{4,3,2,1,0:T(8,128)(2,1)}, u32[]{:S(2)}, u32[]{:S(2)}) %all-to-all-start) | async-done | bytes 4194336 | tf_op jit(solution)/shard_map/all_to_all | solution.py:31
  412.1 1.2 mul.119
  413.4 0.0 copy-start.1
  413.4 3.4 fusion.1
  416.8 0.6 broadcast_multiply_fusion
  417.4 0.0 copy-done.1
  (4 shorter events, 0.1 us)
Async XLA Ops:
  7.2 129.8 %copy-start = (bf16[128,4096]{1,0:T(8,128)(2,1)S(1)}, bf16[128,4096]{1,0:T(8,128)(2,1)}, u32[]{:S(2)}) copy-start(bf16[128,4096]{1,0:T(8,128)(2,1)} %param.4) | copy-start | bytes 3145732
  7.2 129.7 %all-gather.2.cloned.1.call-start = ((), (), s32[]{:S(2)}) async-start(), calls=%async_computation.2 | async-start | bytes 4456448 | tf_op jit(solution)/shard_map/all_gather | solution.py:99
  173.5 36.5 %all-to-all-start.1 = ((bf16[512,1,1,8,2]{3,4,2,1,0:T(2,128)(2,1)}), bf16[512,1,1,8,2]{3,4,2,1,0:T(2,128)(2,1)S(1)}, u32[]{:S(2)}, u32[]{:S(2)}) async-start(bf16[512,1,1,8,2]{3,4,2,1,0:T(2,128)(2,1)} %bitcast.14), calls=%async_computation.1 | async-start | bytes 524288 | tf_op jit(solution)/shard_map/all_to_all | solution.py:31
  210.0 202.2 %all-to-all-start = ((bf16[512,1,1,8,512]{4,3,2,1,0:T(8,128)(2,1)}), bf16[512,1,1,8,512]{4,3,2,1,0:T(8,128)(2,1)}, u32[]{:S(2)}, u32[]{:S(2)}) async-start(bf16[512,1,1,8,512]{4,3,2,1,0:T(8,128)(2,1)} %bitcast.45), calls=%async_computation | async-start | bytes 8388608 | tf_op jit(solution)/shard_map/all_to_all | solution.py:31
  413.4 4.1 copy-start.1
Sparse Core Ops, SparseCore 0:
  11.9 125.0 all-gather.1
where the time goes:
time: 425 us; the launch traced here: 424 us
  waiting for transfers between devices  326 us (77%)
  local copies, waits for them, and re-layouts  34.4 us (8%)
  starting transfers between devices  22.9 us (5%)
  other arithmetic  14.7 us (3%)
  between operations  14.2 us (3%)
  matrix products  12.6 us (3%)
    all_to_all x2, waiting for transfers between devices, joined_exchange(): lax.all_to_all(blocks, axis, split_axis=0, concat_axis=0, tiled=True)  200 us
    all_gather x1, waiting for transfers between devices, on_device(): weights = lax.all_gather(shard_weights, 'local', axis=0, tiled=True)  125 us
    all_to_all x2, starting transfers between devices, joined_exchange(): lax.all_to_all(blocks, axis, split_axis=0, concat_axis=0, tiled=True)  22.8 us
    div x2, local copies, waits for them, and re-layouts, quantize(): code_values = (blocks / block_scale[:, :, None]).astype(jnp.bfloat16)  17.4 us
    dot_general x1, local copies, waits for them, and re-layouts, on_device(): lax.dot_general(tokens, pre_grad, (((0,), (0,)), ((), ())), preferred_ele...  8.99 us
  transfers between devices with their start and end apart: 3, of which 3 were waited for; matrix products, arithmetic and copies ran while one was open for 4% of the time, Pallas kernels for 0%

commit v1 on v0

--- a/solution.py
+++ b/solution.py
@@ -96,7 +96,10 @@
     feature_count = key_codes.shape[1]
     expanded = jnp.repeat(jnp.exp2(key_exponents.astype(jnp.float32)), QBLOCK, axis=1)
     shard_weights = (key_codes.astype(jnp.float32) * expanded).astype(jnp.bfloat16)
-    weights = lax.all_gather(shard_weights, "local", axis=0, tiled=True)
+    n_dev = lax.axis_size("local")
+    pieces = jnp.stack([shard_weights for _ in range(n_dev)])
+    pieces = lax.all_to_all(pieces, "local", split_axis=0, concat_axis=0)
+    weights = jnp.concatenate(pieces, axis=0)
     device_index = lax.axis_index("node") * local_count + lax.axis_index("local")
     positions = (device_index * tok_count + jnp.arange(tok_count, dtype=jnp.int32)) % SEQ
     cosine, sine_part = tables(positions)

time: 425 us -> 476 us (1.12)
  starting transfers between devices: 22.9 us -> 174 us
  waiting for transfers between devices: 326 us -> 237 us
  between operations: 14.2 us -> 0.89 us
    all_to_all x2, starting transfers between devices: 22.8 us -> 169 us  [joined_exchange(): lax.all_to_all(blocks, axis, split_axis=0, concat_axis=0, tiled=True)]
    all_gather x1 -> x0, waiting for transfers between devices: 125 us -> none  [on_device(): weights = lax.all_gather(shard_weights, 'local', axis=0, tiled=True)]
    all_to_all x0 -> x1, waiting for transfers between devices: none -> 30.7 us  [on_device(): pieces = lax.all_to_all(pieces, 'local', split_axis=0, concat_axis=0)]
    all_to_all x2, waiting for transfers between devices: 200 us -> 206 us  [joined_exchange(): lax.all_to_all(blocks, axis, split_axis=0, concat_axis=0, tiled=True)]
  transfers between devices with their start and end apart: 3 -> 3, of which waited for: 3 -> 3; matrix products, arithmetic and copies ran while one was open for 4% -> 10% of each run, Pallas kernels for 0% -> 0%
where the time goes in v1:
time: 476 us; the launch traced here: 475 us
  waiting for transfers between devices  237 us (50%)
  starting transfers between devices  174 us (37%)
  local copies, waits for them, and re-layouts  38.1 us (8%)
  other arithmetic  12.8 us (3%)
  matrix products  12.6 us (3%)
    all_to_all x2, waiting for transfers between devices, joined_exchange(): lax.all_to_all(blocks, axis, split_axis=0, concat_axis=0, tiled=True)  206 us
    all_to_all x2, starting transfers between devices, joined_exchange(): lax.all_to_all(blocks, axis, split_axis=0, concat_axis=0, tiled=True)  169 us
    all_to_all x1, waiting for transfers between devices, on_device(): pieces = lax.all_to_all(pieces, 'local', split_axis=0, concat_axis=0)  30.7 us
    div x2, local copies, waits for them, and re-layouts, quantize(): code_values = (blocks / block_scale[:, :, None]).astype(jnp.bfloat16)  17.4 us
  transfers between devices with their start and end apart: 3, of which 3 were waited for; matrix products, arithmetic and copies ran while one was open for 10% of the time, Pallas kernels for 0%

profile of v1, /device:TPU:1, one launch (start us, length us, event | category | flops | bytes accessed | tf_op | source)
XLA Modules:
  0.0 475.2 jit_solution(875798948008997446)
XLA Ops:
  0.6 0.0 copy-start
  0.7 1.1 copy.32
  1.8 0.2 multiply_cosine_fusion
  2.0 0.0 copy-start.1
  2.0 0.0 copy-start.3
  2.0 0.5 copy-done.1
  2.6 0.0 copy-done.3
  2.6 0.0 copy-done
  2.6 0.0 copy-start.6
  2.6 0.0 copy-start.5
  2.6 4.5 bitcast_reduce_fusion
  7.1 0.7 fusion.5
  7.8 0.3 reshape.205
  8.1 1.0 copy.31
  9.1 24.3 %all-to-all-start.2 = ((bf16[512,1,1,8,2]{3,4,2,1,0:T(2,128)(2,1)}), bf16[512,1,1,8,2]{3,4,2,1,0:T(2,128)(2,1)S(1)}, u32[]{:S(2)}, u32[]{:S(2)}) async-start(bf16[512,1,1,8,2]{3,4,2,1,0:T(2,128)(2,1)} %bitcast.15), calls=%async_computation.2 | async-start | bytes 524288 | tf_op jit(solution)/shard_map/all_to_all | solution.py:31
  33.4 0.0 copy-done.6
  33.5 0.1 copy.20
  33.6 0.3 broadcast_in_dim.2
  34.0 0.0 copy-done.5
  34.0 0.1 multiply_convert_fusion
  34.1 24.3 %all-to-all-done.2 = bf16[512,1,1,8,2]{3,4,2,1,0:T(2,128)(2,1)S(1)} async-done(((bf16[512,1,1,8,2]{3,4,2,1,0:T(2,128)(2,1)}), bf16[512,1,1,8,2]{3,4,2,1,0:T(2,128)(2,1)S(1)}, u32[]{:S(2)}, u32[]{:S(2)}) %all-to-all-start.2) | async-done | bytes 16416 | tf_op jit(solution)/shard_map/all_to_all | solution.py:31
  58.4 2.3 stack.2
  60.7 4.5 all-to-all-start
  65.2 1.4 copy.25
  66.6 6.0 %div.25 = f32[4096,2,256]{2,1,0:T(2,128)} broadcast(f32[4096,2]{1,0:T(8,128)S(1)} %copy.25), dimensions={0,1} | broadcast | bytes 8421376 | tf_op jit(solution)/shard_map/div | solution.py:80
  72.6 11.5 %div.26 = f32[32,16,1,8,512]{4,3,1,0,2:T(8,128)} reshape(f32[4096,2,256]{2,1,0:T(2,128)} %div.25) | data formatting | bytes 16777216 | tf_op jit(solution)/shard_map/div | solution.py:80
  84.0 9.0 %copy.24 = f32[4096,512]{1,0:T(8,128)} copy(f32[4096,512]{0,1:T(8,128)} %get-tuple-element.12) | data formatting | bytes 16777216 | tf_op jit(solution)/shard_map/dot_general | solution.py:107
  93.0 7.6 %fusion.2 = bf16[16,32,1,8,512]{4,3,0,1,2:T(8,128)(2,1)S(1)} fusion(f32[32,16,1,8,512]{4,3,1,0,2:T(8,128)} %bitcast.44, f32[32,16,1,8,512]{4,3,1,0,2:T(8,128)} %div.26), kind=kLoop, calls=%fused_computation.7 | loop fusion | flops 4194304 | bytes 20971520 | tf_op jit(solution)/shard_map/transpose | solution.py:16
  100.6 2.4 copy.26
  103.0 30.7 %all-to-all-done = bf16[16,256,512]{2,1,0:T(8,128)(2,1)} async-done(((bf16[16,256,512]{2,1,0:T(8,128)(2,1)}), bf16[16,256,512]{2,1,0:T(8,128)(2,1)}, u32[]{:S(2)}, u32[]{:S(2)}) %all-to-all-start) | async-done | bytes 4194336 | tf_op jit(solution)/shard_map/all_to_all | solution.py:101
  133.8 145.0 %all-to-all-start.1 = ((bf16[512,1,1,8,512]{4,3,2,1,0:T(8,128)(2,1)}), bf16[512,1,1,8,512]{4,3,2,1,0:T(8,128)(2,1)}, u32[]{:S(2)}, u32[]{:S(2)}) async-start(bf16[512,1,1,8,512]{4,3,2,1,0:T(8,128)(2,1)} %bitcast.46), calls=%async_computation.1 | async-start | bytes 8388608 | tf_op jit(solution)/shard_map/all_to_all | solution.py:31
  278.7 0.0 copy-start.2
  278.7 0.0 copy-start.4
  278.8 0.2 convert_bitcast_fusion.1
  279.0 3.5 fusion.6
  282.4 0.0 copy-done.2
  282.5 0.0 copy-done.4
  282.5 0.8 copy.30
  283.3 4.6 convolution_convert_fusion
  288.0 182.0 %all-to-all-done.1 = bf16[512,1,1,8,512]{4,3,2,1,0:T(8,128)(2,1)} async-done(((bf16[512,1,1,8,512]{4,3,2,1,0:T(8,128)(2,1)}), bf16[512,1,1,8,512]{4,3,2,1,0:T(8,128)(2,1)}, u32[]{:S(2)}, u32[]{:S(2)}) %all-to-all-start.1) | async-done | bytes 4194336 | tf_op jit(solution)/shard_map/all_to_all | solution.py:31
  470.0 1.2 mul.119
  471.2 3.4 fusion.1
  474.5 0.6 broadcast_multiply_fusion
  (8 shorter events, 0.2 us)
Async XLA Ops:
  0.6 2.0 copy-start
  2.0 0.6 copy-start.1
  2.0 0.6 copy-start.3
  2.6 30.8 %copy-start.6 = (s32[256,2]{0,1:T(2,128)S(1)}, s32[256,2]{0,1:T(2,128)}, u32[]{:S(2)}) copy-start(s32[256,2]{0,1:T(2,128)} %param.6) | copy-start | bytes 6148
  2.6 31.3 %copy-start.5 = (bf16[256,512]{1,0:T(8,128)(2,1)S(1)}, bf16[256,512]{1,0:T(8,128)(2,1)}, u32[]{:S(2)}) copy-start(bf16[256,512]{1,0:T(8,128)(2,1)} %param.5) | copy-start | bytes 786436
  9.1 49.3 %all-to-all-start.2 = ((bf16[512,1,1,8,2]{3,4,2,1,0:T(2,128)(2,1)}), bf16[512,1,1,8,2]{3,4,2,1,0:T(2,128)(2,1)S(1)}, u32[]{:S(2)}, u32[]{:S(2)}) async-start(bf16[512,1,1,8,2]{3,4,2,1,0:T(2,128)(2,1)} %bitcast.15), calls=%async_computation.2 | async-start | bytes 524288 | tf_op jit(solution)/shard_map/all_to_all | solution.py:31
  60.7 73.1 %all-to-all-start = ((bf16[16,256,512]{2,1,0:T(8,128)(2,1)}), bf16[16,256,512]{2,1,0:T(8,128)(2,1)}, u32[]{:S(2)}, u32[]{:S(2)}) async-start(bf16[16,256,512]{2,1,0:T(8,128)(2,1)} %stack.2), calls=%async_computation | async-start | bytes 8388608 | tf_op jit(solution)/shard_map/all_to_all | solution.py:101
  133.8 336.2 %all-to-all-start.1 = ((bf16[512,1,1,8,512]{4,3,2,1,0:T(8,128)(2,1)}), bf16[512,1,1,8,512]{4,3,2,1,0:T(8,128)(2,1)}, u32[]{:S(2)}, u32[]{:S(2)}) async-start(bf16[512,1,1,8,512]{4,3,2,1,0:T(8,128)(2,1)} %bitcast.46), calls=%async_computation.1 | async-start | bytes 8388608 | tf_op jit(solution)/shard_map/all_to_all | solution.py:31
  278.7 3.7 copy-start.2
  278.7 3.7 copy-start.4
